TPU v7x, 512 devices: a whole 4x8x8 slice. The times are simulated.
512 devices in a mesh: seq: 64 (over z_lo, x, y), kv: 8 (over z_hi, core).
Axes of the slice: x: 4, y: 8, z: 8 (z_hi: 4, z_lo: 2; z = z_hi * 2 + z_lo), core: 2. Of those that a mesh axis runs over, the one named last changes fastest.
Arguments:
- text_query: bfloat16 [8192, 8192], P('seq', 'kv'), may hold values from -20 to 20, as said below
- vision_key: bfloat16 [2048, 1024], P('seq', 'kv'), may hold values from -4 to 4, as said below
- vision_value: bfloat16 [2048, 1024], P('seq', 'kv'), may hold values from -6 to 6
- grad_output: bfloat16 [8192, 8192], P('seq', 'kv'), may hold values from -192 to 192
- key_weight: bfloat16 [8192, 1024], P('seq', 'kv'), may hold values from -0.1875 to 0.1875
- value_weight: bfloat16 [8192, 1024], P('seq', 'kv'), may hold values from -0.1875 to 0.1875
Outputs:
- grad_query: bfloat16 [8192, 8192], P('seq', 'kv')
- grad_vision: bfloat16 [2048, 8192], P('seq', 'kv')
Inputs may be any that keep to these rules, and one draw needn't show every extreme that they name: `text_query`: entries of order one; some rows of single heads may be large multiples of a key row. `vision_key`: entries of order one.
All inputs are finite; a program needn't handle non-finite values.
Results may differ from a plain program's by a relative error of at most 0.02.
Values may be sent and summed in bfloat16 or wider, within the bound.
A program may use at most 64 MiB of HBM per device.

v0:
```python
import math
import jax
import jax.numpy as jnp
from jax import lax
from jax.sharding import PartitionSpec as P

HEAD = 128


def sweep(block_step, running, shard_piece):
    key_part, value_part = shard_piece
    key_count = key_part.shape[0]
    block_rows = 512
    num_blocks = key_count // block_rows
    key_blocks = key_part.reshape(num_blocks, block_rows, key_part.shape[1])
    value_blocks = value_part.reshape(num_blocks, block_rows, value_part.shape[1])

    def inner(inner_state, inputs):
        key_block, value_block, block_index = inputs
        return (block_step(inner_state, key_block, value_block, block_index * block_rows), None)

    result, unused = lax.scan(
        inner, running, (key_blocks, value_blocks, jnp.arange(num_blocks, dtype=jnp.int32))
    )
    return result


def shards(text_query, vision_key, vision_value, grad_output, key_weight, value_weight):
    scaling = 1.0 / math.sqrt(HEAD)
    row_count = text_query.shape[0]
    head_count = text_query.shape[1] // HEAD
    queries = text_query.reshape(row_count, head_count, HEAD)
    upstream = grad_output.reshape(row_count, head_count, HEAD)
    shard_keys = vision_key.shape[0]
    total_keys = shard_keys * lax.axis_size("seq")

    def logit_pair(key_block, value_block):
        logits = (
            jnp.einsum("thd,kd->htk", queries, key_block, preferred_element_type=jnp.float32)
            * scaling
        )
        grad_probs = jnp.einsum(
            "thd,kd->htk", upstream, value_block, preferred_element_type=jnp.float32
        )
        return (logits, grad_probs)

    def stats_block(running, key_block, value_block, offset):
        row_max, row_sums, weighted = running
        logits, grad_probs = logit_pair(key_block, value_block)
        new_max = jnp.maximum(row_max, jnp.max(logits, axis=2))
        exponent = jnp.exp(logits - new_max[:, :, None])
        factor = jnp.exp(row_max - new_max)
        return (
            new_max,
            row_sums * factor + jnp.sum(exponent, axis=2),
            weighted * factor + jnp.sum(exponent * grad_probs, axis=2),
        )

    init_stats = (
        jnp.full((head_count, row_count), -jnp.inf, jnp.float32),
        jnp.zeros((head_count, row_count), jnp.float32),
        jnp.zeros((head_count, row_count), jnp.float32),
    )

    def make_grads(stats):
        row_max, row_sums, weighted = stats
        row_dots = weighted / row_sums

        def attend(key_block, value_block):
            logits, grad_probs = logit_pair(key_block, value_block)
            attention = jnp.exp(logits - row_max[:, :, None]) / row_sums[:, :, None]
            grad_logits = (attention * (grad_probs - row_dots[:, :, None]) * scaling).astype(
                jnp.bfloat16
            )
            return (attention, grad_logits)

        def block_terms(attention, grad_logits):
            value_term = jnp.einsum(
                "htk,thd->kd",
                attention.astype(jnp.bfloat16),
                upstream,
                preferred_element_type=jnp.float32,
            )
            key_term = jnp.einsum(
                "htk,thd->kd", grad_logits, queries, preferred_element_type=jnp.float32
            )
            return jnp.concatenate([key_term, value_term], axis=1)

        def grad_block(running, key_block, value_block, offset):
            query_grad, key_grads = running
            attention, grad_logits = attend(key_block, value_block)
            query_grad = query_grad + jnp.einsum(
                "htk,kd->thd", grad_logits, key_block, preferred_element_type=jnp.float32
            )
            key_grads = lax.dynamic_update_slice(
                key_grads, block_terms(attention, grad_logits), (offset, jnp.int32(0))
            )
            return (query_grad, key_grads)

        def query_block(query_grad, key_block, value_block, offset):
            attention, grad_logits = attend(key_block, value_block)
            return query_grad + jnp.einsum(
                "htk,kd->thd", grad_logits, key_block, preferred_element_type=jnp.float32
            )

        return (attend, block_terms, grad_block, query_block)

    init_query = jnp.zeros((row_count, head_count, HEAD), jnp.float32)
    init_grads = (init_query, jnp.zeros((total_keys, 2 * HEAD), jnp.float32))
    keys_all, values_all = (
        lax.all_gather(vision_key, "seq", axis=0, tiled=True),
        lax.all_gather(vision_value, "seq", axis=0, tiled=True),
    )
    stats = sweep(stats_block, init_stats, (keys_all, values_all))
    attend, block_terms, grad_block, query_block = make_grads(stats)
    query_grad, key_grads = sweep(grad_block, init_grads, (keys_all, values_all))
    owned_sums = lax.psum_scatter(key_grads, "seq", scatter_dimension=0, tiled=True)
    owned_grads = owned_sums.astype(jnp.bfloat16)
    merged_weights = jnp.concatenate([key_weight, value_weight], axis=1)
    vision_terms = jnp.einsum(
        "kc,rc->kr",
        owned_grads,
        lax.all_gather(merged_weights, "seq", axis=0, tiled=True),
        preferred_element_type=jnp.float32,
    )
    grad_vision = lax.psum_scatter(
        vision_terms.astype(jnp.bfloat16), "kv", scatter_dimension=1, tiled=True
    )
    grad_query = query_grad.reshape(row_count, head_count * HEAD).astype(jnp.bfloat16)
    return (grad_query, grad_vision)


def solution(mesh):
    return jax.shard_map(
        shards,
        mesh=mesh,
        in_specs=(
            P("seq", "kv"),
            P("seq", "kv"),
            P("seq", "kv"),
            P("seq", "kv"),
            P("seq", "kv"),
            P("seq", "kv"),
        ),
        out_specs=(P("seq", "kv"), P("seq", "kv")),
        check_vma=False,
    )
```

profile of v0, /device:TPU:10, one launch (start us, length us, event | category | flops | bytes accessed | tf_op | source)
XLA Modules:
  0.0 1057.6 jit_solution(18121476715610056676)
XLA Ops:
  7.3 153.0 %all_gather.9 = bf16[2048,128]{1,0:T(8,128)(2,1)} all-gather(bf16[32,128]{1,0:T(8,128)(2,1)} %param.11), channel_id=1, replica_groups=mesh['seq'=64,'kv'=8] {'seq'}, dimensions={0}, use_global_device_ids=true | all-gather | bytes 532480 | tf_op jit(solution)/shard_map/all_gather | solution.py:111
  160.2 164.7 %all_gather.10 = bf16[2048,128]{1,0:T(8,128)(2,1)} all-gather(bf16[32,128]{1,0:T(8,128)(2,1)} %param.12), channel_id=1, replica_groups=mesh['seq'=64,'kv'=8] {'seq'}, dimensions={0}, use_global_device_ids=true | all-gather | bytes 532480 | tf_op jit(solution)/shard_map/all_gather | solution.py:112
  324.9 1.1 copy.25
  326.4 0.9 copy.28
  327.2 13.4 %while.28 = (s32[]{:T(128)}, f32[8,128]{1,0:T(8,128)S(1)}, f32[8,128]{1,0:T(8,128)S(1)}, f32[8,128]{1,0:T(8,128)S(1)}, bf16[4,512,128]{2,1,0:T(8,128)(2,1)}, /*i...) while((s32[]{:T(128)}, f32[8,128]{1,0:T(8,128)S(1)}, ...), condition=%wide.region_4.5_spmd.clone, body=%wide.region_0.4_spmd.clone.sunk | while | flops 273161216 | bytes 7152752 | solution.py:22
  327.2 1.3 bitcast_reduce_fusion.2
  328.6 1.6 fusion.61
  330.6 1.3 bitcast_reduce_fusion.2
  332.0 1.6 fusion.61
  334.0 1.3 bitcast_reduce_fusion.2
  335.3 1.6 fusion.61
  337.3 1.3 bitcast_reduce_fusion.2
  338.7 1.6 fusion.61
  340.7 1.5 broadcast_in_dim.14.clone
  342.1 29.6 %while.29 = (s32[]{:T(128)}, f32[128,8,128]{0,2,1:T(8,128)S(1)}, f32[2048,256]{1,0:T(8,128)}, bf16[4,512,128]{2,1,0:T(8,128)(2,1)}, bf16[128,8,128]{0,2,1:T(8,12...) while((s32[]{:T(128)}, f32[128,8,128]{0,2,1:T(8,128)S(1)}, ...), condition=%wide.region_6.7_spmd.clone, body=%wide.region_5.6_spmd.clone.sunk | while | flops 675676160 | bytes 15611605 | solution.py:22
  342.1 1.4 fusion.74
  343.6 1.3 fusion.75
  348.2 1.3 fusion.76
  349.5 1.4 fusion.74
  351.0 1.3 fusion.75
  355.6 1.3 fusion.76
  356.9 1.4 fusion.74
  358.4 1.3 fusion.75
  363.0 1.3 fusion.76
  364.4 1.4 fusion.74
  365.8 1.3 fusion.75
  370.4 1.3 fusion.76
  373.2 311.3 %reduce-scatter.7.cloned.1.call-done = f32[32,256]{1,0:T(8,128)} async-done(((f32[2048,256]{1,0:T(8,128)}), f32[32,256]{1,0:T(8,128)}) %reduce-scatter.7.cloned.1.call-update) | async-done | bytes 32784
  684.6 0.9 copy.39
  685.5 308.7 %all-gather.2.cloned.1.call-done = bf16[8192,256]{1,0:T(8,128)(2,1)} async-done(((bf16[128,256]{1,0:T(8,128)(2,1)}), bf16[8192,256]{1,0:T(8,128)(2,1)}) %all-gather.2.cloned.1.call-update) | async-done | bytes 4194320 | tf_op jit(solution)/shard_map/all_gather | solution.py:123
  994.1 4.3 convolution_convert_fusion
  999.4 51.7 %reduce-scatter.5.cloned.1.call-done = bf16[32,1024]{1,0:T(8,128)(2,1)} async-done(((bf16[32,8192]{1,0:T(8,128)(2,1)}), bf16[32,1024]{1,0:T(8,128)(2,1)}) %reduce-scatter.5.cloned.1.call-update) | async-done | bytes 65552 | tf_op jit(solution)/shard_map/reduce_scatter | solution.py:126
  (63 shorter events, 14.7 us)
Async XLA Ops:
  7.2 319.0 %copy-start = (bf16[128,1024]{1,0:T(8,128)(2,1)S(1)}, bf16[128,1024]{1,0:T(8,128)(2,1)}, u32[]{:S(2)}) copy-start(bf16[128,1024]{1,0:T(8,128)(2,1)} %param.13) | copy-start | bytes 786436
  7.2 677.4 %reduce-scatter.7.cloned.1.call-start = ((), (), s32[]{:S(2)}) async-start(), calls=%async_computation.4 | async-start | bytes 2129920
  371.8 0.8 copy-start.1
  371.8 0.8 copy-start.2
  371.8 622.3 %all-gather.2.cloned.1.call-start = ((), (), s32[]{:S(2)}) async-start(), calls=%async_computation.2 | async-start | bytes 4259840 | tf_op jit(solution)/shard_map/all_gather | solution.py:123
  373.2 677.9 %reduce-scatter.5.cloned.1.call-start = ((), (), s32[]{:S(2)}) async-start(), calls=%async_computation.3 | async-start | bytes 589824 | tf_op jit(solution)/shard_map/reduce_scatter | solution.py:126
Sparse Core Ops, SparseCore 0:
  371.9 312.6 reduce-scatter.6
  687.4 306.6 all-gather.1
  998.6 52.4 reduce-scatter.4
where the time goes:
time: 1060 us
  waiting for transfers between devices  672 us (63%)
  blocking collectives  318 us (30%)
  matrix products  36.1 us (3%)
  between operations  13.9 us (1%)
  local copies, waits for them, and re-layouts  12.7 us (1%)
    unnamed x4, waiting for transfers between devices  311 us
    all_gather x1, waiting for transfers between devices, shards(): lax.all_gather(merged_weights, 'seq', axis=0, tiled=True)  309 us
    all_gather x1, blocking collectives, shards(): lax.all_gather(vision_value, 'seq', axis=0, tiled=True)  165 us
    all_gather x1, blocking collectives, shards(): lax.all_gather(vision_key, 'seq', axis=0, tiled=True)  153 us
    reduce_scatter x1, waiting for transfers between devices, shards(): lax.psum_scatter(vision_terms.astype(jnp.bfloat16), 'kv', scatter_dimensi...  51.7 us
  transfers between devices with their start and end apart: 3, of which 3 were waited for; matrix products, arithmetic and copies ran while one was open for 0% of the time, Pallas kernels for 0%

commit v1 on v0

--- a/solution.py
+++ b/solution.py
@@ -3,6 +3,7 @@
 import jax.numpy as jnp
 from jax import lax
 from jax.sharding import PartitionSpec as P
+from jax.lax import all_to_all, axis_size
 
 HEAD = 128
 
@@ -108,7 +109,10 @@
     init_query = jnp.zeros((row_count, head_count, HEAD), jnp.float32)
     init_grads = (init_query, jnp.zeros((total_keys, 2 * HEAD), jnp.float32))
     keys_all, values_all = (
-        lax.all_gather(vision_key, "seq", axis=0, tiled=True),
+        jnp.concatenate(
+            all_to_all(jnp.stack([vision_key for _ in range(axis_size("seq"))]), "seq", 0, 0),
+            axis=0,
+        ),
         lax.all_gather(vision_value, "seq", axis=0, tiled=True),
     )
     stats = sweep(stats_block, init_stats, (keys_all, values_all))

time: 1060 us -> 908 us (0.86)
  the two profiles are of different devices: /device:TPU:10 before, /device:TPU:4 now
where the time goes in v1:
time: 908 us; the launch traced here: 907 us
  waiting for transfers between devices  686 us (76%)
  blocking collectives  138 us (15%)
  matrix products  36.1 us (4%)
  local copies, waits for them, and re-layouts  14.4 us (2%)
  between operations  13.9 us (2%)
  starting transfers between devices  12.8 us (1%)
    unnamed x4, waiting for transfers between devices  316 us
    all_gather x1, waiting for transfers between devices, shards(): lax.all_gather(merged_weights, 'seq', axis=0, tiled=True)  309 us
    all_gather x1, blocking collectives, shards(): lax.all_gather(vision_value, 'seq', axis=0, tiled=True)  138 us
    reduce_scatter x1, waiting for transfers between devices, shards(): lax.psum_scatter(vision_terms.astype(jnp.bfloat16), 'kv', scatter_dimensi...  61.6 us
  transfers between devices with their start and end apart: 4, of which 3 were waited for; matrix products, arithmetic and copies ran while one was open for 1% of the time, Pallas kernels for 0%

profile of v1, /device:TPU:4, one launch (start us, length us, event | category | flops | bytes accessed | tf_op | source)
XLA Modules:
  0.0 907.0 jit_solution(5646922172856059942)
XLA Ops:
  7.2 1.6 stack.2
  8.8 12.6 %all-to-all-start = ((bf16[64,32,128]{2,1,0:T(8,128)(2,1)}), bf16[64,32,128]{2,1,0:T(8,128)(2,1)}, u32[]{:S(2)}, u32[]{:S(2)}) async-start(bf16[64,32,128]{2,1,0:T(8,128)(2,1)} %stack.2), calls=%async_computation | async-start | bytes 1048576 | tf_op jit(solution)/shard_map/all_to_all | solution.py:113
  21.5 1.1 copy.25
  23.9 138.3 %all_gather.6 = bf16[2048,128]{1,0:T(8,128)(2,1)} all-gather(bf16[32,128]{1,0:T(8,128)(2,1)S(1)} %copy-done.3), channel_id=1, replica_groups=mesh['seq'=64,'kv'=8] {'seq'}, dimensions={0}, use_global_device_ids=true | all-gather | bytes 532480 | tf_op jit(solution)/shard_map/all_gather | solution.py:116
  162.2 13.4 %while.28 = (s32[]{:T(128)}, f32[8,128]{1,0:T(8,128)S(1)}, f32[8,128]{1,0:T(8,128)S(1)}, f32[8,128]{1,0:T(8,128)S(1)}, bf16[4,512,128]{2,1,0:T(8,128)(2,1)}, /*i...) while((s32[]{:T(128)}, f32[8,128]{1,0:T(8,128)S(1)}, ...), condition=%wide.region_4.5_spmd.clone, body=%wide.region_0.4_spmd.clone.sunk | while | flops 273161216 | bytes 7152752 | solution.py:23
  162.2 1.3 bitcast_reduce_fusion.2
  163.6 1.6 fusion.61
  165.6 1.3 bitcast_reduce_fusion.2
  167.0 1.6 fusion.61
  168.9 1.3 bitcast_reduce_fusion.2
  170.3 1.6 fusion.61
  172.3 1.3 bitcast_reduce_fusion.2
  173.7 1.6 fusion.61
  175.7 1.5 broadcast_in_dim.14.clone
  177.1 29.6 %while.29 = (s32[]{:T(128)}, f32[128,8,128]{0,2,1:T(8,128)S(1)}, f32[2048,256]{1,0:T(8,128)}, bf16[4,512,128]{2,1,0:T(8,128)(2,1)}, bf16[128,8,128]{0,2,1:T(8,12...) while((s32[]{:T(128)}, f32[128,8,128]{0,2,1:T(8,128)S(1)}, ...), condition=%wide.region_6.7_spmd.clone, body=%wide.region_5.6_spmd.clone.sunk | while | flops 675676160 | bytes 15611605 | solution.py:23
  177.1 1.4 fusion.74
  178.6 1.3 fusion.75
  183.2 1.3 fusion.76
  184.6 1.4 fusion.74
  186.0 1.3 fusion.75
  190.6 1.3 fusion.76
  192.0 1.4 fusion.74
  193.4 1.3 fusion.75
  198.1 1.3 fusion.76
  199.4 1.4 fusion.74
  200.8 1.3 fusion.75
  205.5 1.3 fusion.76
  208.3 315.7 %reduce-scatter.7.cloned.1.call-done = f32[32,256]{1,0:T(8,128)} async-done(((f32[2048,256]{1,0:T(8,128)}), f32[32,256]{1,0:T(8,128)}) %reduce-scatter.7.cloned.1.call-update) | async-done | bytes 32784
  524.0 0.9 copy.39
  524.9 308.8 %all-gather.2.cloned.1.call-done = bf16[8192,256]{1,0:T(8,128)(2,1)} async-done(((bf16[128,256]{1,0:T(8,128)(2,1)}), bf16[8192,256]{1,0:T(8,128)(2,1)}) %all-gather.2.cloned.1.call-update) | async-done | bytes 4194320 | tf_op jit(solution)/shard_map/all_gather | solution.py:127
  833.7 4.4 convolution_convert_fusion
  839.0 61.6 %reduce-scatter.5.cloned.1.call-done = bf16[32,1024]{1,0:T(8,128)(2,1)} async-done(((bf16[32,8192]{1,0:T(8,128)(2,1)}), bf16[32,1024]{1,0:T(8,128)(2,1)}) %reduce-scatter.5.cloned.1.call-update) | async-done | bytes 65552 | tf_op jit(solution)/shard_map/reduce_scatter | solution.py:130
  (67 shorter events, 15.6 us)
Async XLA Ops:
  7.2 15.7 %copy-start = (bf16[128,1024]{1,0:T(8,128)(2,1)S(1)}, bf16[128,1024]{1,0:T(8,128)(2,1)}, u32[]{:S(2)}) copy-start(bf16[128,1024]{1,0:T(8,128)(2,1)} %param.13) | copy-start | bytes 786436
  7.2 16.7 %copy-start.3 = (bf16[32,128]{1,0:T(8,128)(2,1)S(1)}, bf16[32,128]{1,0:T(8,128)(2,1)}, u32[]{:S(2)}) copy-start(bf16[32,128]{1,0:T(8,128)(2,1)} %param.12) | copy-start | bytes 24580
  8.8 153.4 %all-to-all-start = ((bf16[64,32,128]{2,1,0:T(8,128)(2,1)}), bf16[64,32,128]{2,1,0:T(8,128)(2,1)}, u32[]{:S(2)}, u32[]{:S(2)}) async-start(bf16[64,32,128]{2,1,0:T(8,128)(2,1)} %stack.2), calls=%async_computation | async-start | bytes 1048576 | tf_op jit(solution)/shard_map/all_to_all | solution.py:113
  21.4 502.6 %reduce-scatter.7.cloned.1.call-start = ((), (), s32[]{:S(2)}) async-start(), calls=%async_computation.5 | async-start | bytes 2129920
  206.8 0.8 copy-start.1
  206.8 0.8 copy-start.2
  206.8 626.8 %all-gather.2.cloned.1.call-start = ((), (), s32[]{:S(2)}) async-start(), calls=%async_computation.3 | async-start | bytes 4259840 | tf_op jit(solution)/shard_map/all_gather | solution.py:127
  208.2 692.3 %reduce-scatter.5.cloned.1.call-start = ((), (), s32[]{:S(2)}) async-start(), calls=%async_computation.4 | async-start | bytes 589824 | tf_op jit(solution)/shard_map/reduce_scatter | solution.py:130
Sparse Core Ops, SparseCore 0:
  207.0 317.0 reduce-scatter.6
  526.9 306.7 all-gather.1
  838.2 62.2 reduce-scatter.4
